TPU v7x, 256 devices: a whole 4x4x8 slice. The times are simulated.
256 devices in a mesh: dp: 16 (over y, x), fsdp: 16 (over z, core).
Axes of the slice: x: 4, y: 4, z: 8, core: 2. Of those that a mesh axis runs over, the one named last changes fastest.
Arguments:
- grads: bfloat16 [16, 16, 1408, 2048], P('dp', None, 'fsdp')
- momentum: float32 [16, 1408, 2048], P(None, 'fsdp', 'dp')
- weights: bfloat16 [16, 1408, 2048], P(None, 'fsdp', 'dp'), may hold values from -0.125 to 0.125
Outputs:
- moment_new: float32 [16, 1408, 2048], P(None, 'fsdp', 'dp')
- new_weights: bfloat16 [16, 1408, 2048], P(None, 'fsdp', 'dp')
- update: bfloat16 [16, 1408, 2048], P(None, 'fsdp', 'dp')
All inputs are finite; a program needn't handle non-finite values.
Results may differ from a plain program's by a relative error of at most 0.03.
Values may be sent and summed in bfloat16 or wider, within the bound.
No kernel may reach another device: no remote copies, remote signals or barrier semaphores. Data moves between devices by JAX's collectives and lax.ppermute only.
A program may use at most 64 MiB of HBM per device.

v0:
```python
import math

import jax
import jax.numpy as jnp
from jax import lax
from jax.sharding import PartitionSpec as P

NS_ITERS = 2


MOMENTUM_DECAY = 0.95
LEARN_RATE = 0.02
DECAY_RATE = 0.1
COEF_A = 3.4445
COEF_B = -4.775
COEF_C = 2.0315
EPS_NORM = 1e-07


def body(grads, momentum, weights):
    owner_count = lax.axis_size("fsdp")
    group_count = lax.axis_size("dp")
    mat_count, rows_dev, cols_dev = momentum.shape
    rows_total = rows_dev * owner_count
    cols_total = cols_dev * group_count
    summed = lax.psum_scatter(
        grads.astype(jnp.float32).astype(jnp.bfloat16), "dp", scatter_dimension=3, tiled=True
    ).astype(jnp.float32)[0]
    moment_new = MOMENTUM_DECAY * momentum + summed
    sent = moment_new.astype(jnp.bfloat16)
    arrived = lax.all_to_all(sent, "fsdp", split_axis=0, concat_axis=0, tiled=True).reshape(
        rows_total, cols_dev
    )
    wide = arrived.astype(jnp.float32)
    total = lax.psum(jnp.sum(wide * wide), "dp")
    current = (wide / (jnp.sqrt(total) + EPS_NORM)).astype(jnp.bfloat16)
    for step in range(NS_ITERS):
        term = jnp.dot(current, current.T, preferred_element_type=jnp.float32)
        gram = lax.psum(term.astype(jnp.bfloat16), "dp")
        once = jnp.dot(gram, current, preferred_element_type=jnp.float32).astype(jnp.bfloat16)
        twice = jnp.dot(gram, once, preferred_element_type=jnp.float32)
        current = (
            COEF_A * current.astype(jnp.float32)
            + COEF_B * once.astype(jnp.float32)
            + COEF_C * twice
        ).astype(jnp.bfloat16)
    returned = lax.all_to_all(
        current.reshape(owner_count, rows_dev, cols_dev),
        "fsdp",
        split_axis=0,
        concat_axis=0,
        tiled=True,
    )
    scale = 0.2 * math.sqrt(max(rows_total, cols_total))
    direction = scale * returned.astype(jnp.float32)
    new_weights = (
        weights.astype(jnp.float32) * (1.0 - LEARN_RATE * DECAY_RATE) - LEARN_RATE * direction
    ).astype(jnp.bfloat16)
    return (moment_new, new_weights, direction.astype(jnp.bfloat16))


def solution(mesh):
    placed = (P("dp", None, "fsdp", None), P(None, "fsdp", "dp"), P(None, "fsdp", "dp"))
    return jax.shard_map(
        body,
        mesh=mesh,
        in_specs=placed,
        out_specs=(P(None, "fsdp", "dp"), P(None, "fsdp", "dp"), P(None, "fsdp", "dp")),
        check_vma=False,
    )
```

profile of v0, /device:TPU:64, one launch (start us, length us, event | category | flops | bytes accessed | tf_op | source)
XLA Modules:
  0.0 443.5 jit_solution(17748752463228692638)
XLA Ops:
  7.2 0.0 reduce-scatter.4.cloned.1.call-start
  7.2 11.8 %copy.6 = bf16[1,16,88,2048]{2,1,0,3:T(8,128)(2,1)} copy(bf16[1,16,88,2048]{3,2,1,0:T(8,128)(2,1)} %param.3) | data formatting | bytes 11534336
  19.1 14.4 %reshape.18 = bf16[2048,1408]{1,0:T(8,128)(2,1)} reshape(bf16[2048,1,16,88]{3,2,1,0:T(8,128)(2,1)} %bitcast.22) | data formatting | bytes 11534336
  33.5 0.0 copy-start
  33.5 0.0 reduce-scatter.4.cloned.1.call-update
  33.5 0.0 all-reduce.3.cloned.1.call-start
  33.6 87.4 %reduce-scatter.4.cloned.1.call-done = bf16[128,1408]{1,0:T(8,128)(2,1)} async-done(((bf16[2048,1408]{1,0:T(8,128)(2,1)}), bf16[128,1408]{1,0:T(8,128)(2,1)}) %reduce-scatter.4.cloned.1.call-update) | async-done | bytes 360464
  120.9 2.1 reshape.19
  123.0 0.5 copy.7
  123.5 0.0 copy-done
  123.5 1.0 fusion.9
  124.5 18.9 %all_to_all.10 = bf16[16,88,128]{2,1,0:T(8,128)(2,1)S(1)} all-to-all(bf16[16,88,128]{2,1,0:T(8,128)(2,1)S(1)} %get-tuple-element.3), channel_id=1, replica_groups=mesh['dp'=16,'fsdp'=16] {'fsdp'}, dimensions={0} | all-to-all | bytes 720896 | tf_op jit(solution)/shard_map/all_to_all | solution.py:31
  143.3 0.8 fusion.4
  144.1 38.8 %psum.21 = f32[]{:T(128)} all-reduce(f32[]{:T(128)} %fusion.4), channel_id=1, replica_groups=mesh['dp'=16,'fsdp'=16] {'dp'}, use_global_device_ids=true, to_apply=%region_2.0 | all-reduce | flops 1 | bytes 8 | tf_op jit(solution)/shard_map/psum | solution.py:35
  183.6 0.1 fusion.5
  183.6 3.1 convolution_convert_fusion.1
  186.7 0.0 all-reduce.3.cloned.1.call-update
  186.8 0.0 all-reduce.5.cloned.1.call-start
  186.8 106.0 %all-reduce.3.cloned.1.call-done = bf16[1408,1408]{1,0:T(8,128)(2,1)} async-done(((bf16[1408,1408]{1,0:T(8,128)(2,1)}), bf16[1408,1408]{1,0:T(8,128)(2,1)}) %all-reduce.3.cloned.1.call-update) | async-done | bytes 3964944 | tf_op jit(solution)/shard_map/psum | solution.py:39
  292.8 0.0 copy-start.2
  292.8 3.5 convolution_convert_fusion.3
  296.3 0.0 copy-done.2
  296.3 1.2 fusion.3
  297.6 3.1 convolution_convert_fusion
  300.7 0.0 all-reduce.5.cloned.1.call-update
  300.7 111.6 %all-reduce.5.cloned.1.call-done = bf16[1408,1408]{1,0:T(8,128)(2,1)} async-done(((bf16[1408,1408]{1,0:T(8,128)(2,1)}), bf16[1408,1408]{1,0:T(8,128)(2,1)}) %all-reduce.5.cloned.1.call-update) | async-done | bytes 3964944 | tf_op jit(solution)/shard_map/psum | solution.py:39
  412.3 0.0 copy-start.3
  412.3 3.5 convolution_convert_fusion.2
  415.8 0.0 copy-done.3
  415.8 0.0 copy-start.1
  415.8 1.2 fusion.2
  417.1 18.9 %all_to_all.11 = bf16[16,88,128]{2,1,0:T(8,128)(2,1)S(1)} all-to-all(bf16[16,88,128]{2,1,0:T(8,128)(2,1)S(1)} %bitcast.27), channel_id=1, replica_groups=mesh['dp'=16,'fsdp'=16] {'fsdp'}, dimensions={0} | all-to-all | bytes 720896 | tf_op jit(solution)/shard_map/all_to_all | solution.py:47
  435.9 0.0 copy-done.1
  435.9 1.1 fusion.8
Async XLA Ops:
  7.2 113.8 %reduce-scatter.4.cloned.1.call-start = ((), (), s32[]{:S(2)}) async-start(), calls=%async_computation.5 | async-start | bytes 6127616
  33.5 90.0 %copy-start = (f32[16,88,128]{2,1,0:T(8,128)S(1)}, f32[16,88,128]{2,1,0:T(8,128)}, u32[]{:S(2)}) copy-start(f32[16,88,128]{2,1,0:T(8,128)} %param.4) | copy-start | bytes 2162692
  33.5 259.3 %all-reduce.3.cloned.1.call-start = ((), (), s32[]{:S(2)}) async-start(), calls=%async_computation.3 | async-start | bytes 7929856 | tf_op jit(solution)/shard_map/psum | solution.py:39
  186.8 225.6 %all-reduce.5.cloned.1.call-start = ((), (), s32[]{:S(2)}) async-start(), calls=%async_computation.4 | async-start | bytes 7929856 | tf_op jit(solution)/shard_map/psum | solution.py:39
  292.8 3.5 copy-start.2
  412.3 3.5 copy-start.3
  415.8 20.1 %copy-start.1 = (bf16[16,88,128]{2,1,0:T(8,128)(2,1)S(1)}, bf16[16,88,128]{2,1,0:T(8,128)(2,1)}, u32[]{:S(2)}) copy-start(bf16[16,88,128]{2,1,0:T(8,128)(2,1)} %param.5) | copy-start | bytes 1081348
Sparse Core Ops, SparseCore 0:
  33.6 87.2 reduce-scatter.3
  186.9 105.8 all-reduce.2
  300.8 111.4 all-reduce.4
where the time goes:
time: 448 us; the launch traced here: 444 us
  waiting for transfers between devices  305 us (68%)
  blocking collectives  76.5 us (17%)
  local copies, waits for them, and re-layouts  28.8 us (6%)
  matrix products  15.6 us (3%)
  between operations  14.5 us (3%)
    psum x2, waiting for transfers between devices, body(): gram = lax.psum(term.astype(jnp.bfloat16), 'dp')  218 us
    unnamed x4, waiting for transfers between devices  87.4 us
    psum x1, blocking collectives, body(): total = lax.psum(jnp.sum(wide * wide), 'dp')  38.8 us
    unnamed x12, local copies, waits for them, and re-layouts  28.8 us
    all_to_all x1, blocking collectives, body(): lax.all_to_all(current.reshape(owner_count, rows_dev, cols_dev), 'fsdp',...  18.9 us
    all_to_all x1, blocking collectives, body(): lax.all_to_all(sent, 'fsdp', split_axis=0, concat_axis=0, tiled=True)  18.9 us
  transfers between devices with their start and end apart: 3, of which 3 were waited for; matrix products, arithmetic and copies ran while one was open for 0% of the time, Pallas kernels for 0%

commit v1 on v0

v1 whole, which is shorter than its diff:
```python
import functools
import math

import jax
import jax.numpy as jnp
from jax import lax
from jax.experimental import pallas as pl
from jax.experimental.pallas import tpu as pltpu
from jax.sharding import PartitionSpec as P

NS_ITERS = 2
SIDE = 4
RING = 8
PIECES = RING + 1
LANE = 128
HALVES = 2

MOMENTUM_DECAY = 0.95
LEARN_RATE = 0.02
DECAY_RATE = 0.1
COEF_A = 3.4445
COEF_B = -4.775
COEF_C = 2.0315
EPS_NORM = 1e-07
F32 = jnp.float32
BF16 = jnp.bfloat16
ROWS_BY_ROWS = (((1,), (1,)), ((), ()))
ANYWHERE = pl.BlockSpec(memory_space=pl.ANY)
IN_HBM = pl.BlockSpec(memory_space=pltpu.HBM)
IN_VMEM = pl.BlockSpec(memory_space=pltpu.VMEM)


def move(value, target):
    pairs = []
    for y in range(SIDE):
        for x in range(SIDE):
            for z in range(RING):
                for core in range(2):
                    ty, tx, tz, tc = target(y, x, z, core)
                    there = (((ty % SIDE) * SIDE + tx % SIDE) * RING + tz % RING) * 2 + tc % 2
                    pairs.append((((y * SIDE + x) * RING + z) * 2 + core, there))
    return lax.ppermute(value, ("dp", "fsdp"), pairs)


def first_hop(value, k):
    return move(value, lambda y, x, z, c: (y, x + k, z, c) if c == 0 else (y + k, x, z, c))


def second_hop(value, k):
    return move(value, lambda y, x, z, c: (y + k, x, z, c) if c == 0 else (y, x + k, z, c))


def along_z(value, k):
    return move(value, lambda y, x, z, c: (y, x, z + k, c) if c == 0 else (y, x, z - k, c))


def swap(value):
    return move(value, lambda y, x, z, c: (y, x, z, c + 1))


def cost(flops, size):
    return pl.CostEstimate(flops=flops, bytes_accessed=size, transcendentals=0)


def matrix(k, m):
    place = lax.axis_index("dp")
    y, x = place // SIDE, place % SIDE
    by_x = ((y + m) % SIDE) * SIDE + (x + k) % SIDE
    by_y = ((y + k) % SIDE) * SIDE + (x + m) % SIDE
    return jnp.where(lax.axis_index("fsdp") % 2 == 0, by_x, by_y)


def pack_kernel(wide, wanted, grads, mom, *refs):
    outs, terms, sems = refs[:-2], refs[-2], refs[-1]
    place = lax.axis_index("dp")
    per = wide // LANE
    cols = pl.ds(pl.multiple_of((place % per) * LANE, LANE), LANE)
    copies = []
    for i, (k, half) in enumerate(wanted):
        for m in range(SIDE):
            block = grads.at[0, matrix(k, m), :, pl.ds(half * wide, wide)]
            copies.append(pltpu.make_async_copy(block, outs[i].at[m], sems.at[0, i, m]))
            copies.append(pltpu.make_async_copy(mom.at[matrix(k, m)], terms.at[i, m], sems.at[1, i, m]))
    for copy in copies:
        copy.start()
    for copy in copies:
        copy.wait()
    for i, (_, half) in enumerate(wanted):

        @pl.when(place // per == half)
        def _():
            for m in range(SIDE):
                moment = MOMENTUM_DECAY * terms[i, m] + outs[i][m, :, cols].astype(F32)
                outs[i][m, :, cols] = moment.astype(BF16)


def pack(grads, momentum, wide, wanted, limit):
    rows = grads.shape[2]
    return pl.pallas_call(
        functools.partial(pack_kernel, wide, wanted),
        out_shape=(jax.ShapeDtypeStruct((SIDE, rows, wide), BF16),) * len(wanted),
        in_specs=[IN_HBM, IN_HBM],
        out_specs=(IN_VMEM,) * len(wanted),
        scratch_shapes=[
            pltpu.VMEM((len(wanted), SIDE, rows, LANE), F32),
            pltpu.SemaphoreType.DMA((2, len(wanted), SIDE)),
        ],
        compiler_params=pltpu.CompilerParams(vmem_limit_bytes=limit << 20),
        cost_estimate=cost(0, 4 * SIDE * rows * wide * len(wanted)),
    )(grads, momentum)


def add_kernel(count, split, *refs):
    inputs, outs = refs[: len(refs) - count[1]], refs[len(refs) - count[1] :]
    each = count[0]
    for place in range(len(inputs) // each):
        terms = inputs[place * each : (place + 1) * each]
        for m in range(SIDE):
            total = terms[0][m].astype(F32)
            for term in terms[1:]:
                total = total + term[m].astype(F32)
            if split:
                outs[place * SIDE + m][...] = total.astype(BF16)
            else:
                outs[place][m] = total.astype(BF16)


def add_up(groups, split):
    _, rows, wide = groups[0][0].shape
    if split:
        shape = (jax.ShapeDtypeStruct((rows, wide), BF16),) * (SIDE * len(groups))
    else:
        shape = (jax.ShapeDtypeStruct((SIDE, rows, wide), BF16),) * len(groups)
    inputs = [array for group in groups for array in group]
    return pl.pallas_call(
        functools.partial(add_kernel, (len(groups[0]), len(shape)), split),
        out_shape=shape,
        in_specs=[IN_VMEM] * len(inputs),
        out_specs=(IN_VMEM,) * len(shape),
        compiler_params=pltpu.CompilerParams(vmem_limit_bytes=16 << 20),
        cost_estimate=cost(0, 2 * SIDE * rows * wide * (len(inputs) + len(groups))),
    )(*inputs)


def combine_kernel(part0, part1, part2, part3, blocks, sent):
    for block in range(blocks.shape[0]):
        cols = slice(block * LANE, (block + 1) * LANE)
        total = part0[:, cols].astype(F32) + part1[:, cols].astype(F32)
        total = total + (part2[:, cols].astype(F32) + part3[:, cols].astype(F32))
        rounded = total.astype(BF16)
        blocks[block] = rounded
        sent[:, cols] = rounded


def combine(parts):
    rows, wide = parts[0].shape
    return pl.pallas_call(
        combine_kernel,
        out_shape=(
            jax.ShapeDtypeStruct((wide // LANE, rows, LANE), BF16),
            jax.ShapeDtypeStruct((rows, wide), BF16),
        ),
        in_specs=[IN_VMEM] * SIDE,
        out_specs=(IN_VMEM,) * 2,
        compiler_params=pltpu.CompilerParams(vmem_limit_bytes=16 << 20),
        cost_estimate=cost(0, 12 * rows * wide),
    )(*parts)


def gather(sent, core):
    rows, wide = sent.shape
    other = swap(sent)
    chip = jnp.concatenate([jnp.where(core == 0, sent, other), jnp.where(core == 0, other, sent)], axis=0)
    one = along_z(chip, 1)
    two = along_z(one, 1)
    three = along_z(two, 1)
    four = along_z(lax.dynamic_slice_in_dim(three, core * (wide // 2), wide // 2, axis=1), 1)
    return [chip, one, swap(one), two, swap(two), three, swap(three), four, swap(four)]


def fetch(groups, places, target, first, sems):
    core = lax.axis_index("fsdp") % 2
    copies = []
    for index, group in enumerate(groups):
        high, wide = group[0].shape[0], target.shape[1] // HALVES
        for piece, place in zip(group, places):
            row, width, start = min(place, RING - 1) * high, wide, index * wide
            if place >= RING - 1:
                width = wide // 2
                right = core if place == RING - 1 else 1 - core
                start = pl.multiple_of(start + right * width, LANE)
            into = target.at[pl.ds(row - first, high), pl.ds(start, width)]
            copies.append(pltpu.make_async_copy(piece, into, sems.at[index, place]))
    for copy in copies:
        copy.start()
    for copy in copies:
        copy.wait()


def gram_strips(rows, gram, start, stop):
    for at in range(start, stop, 256):
        end = min(at + 256, stop)
        term = lax.dot_general(
            rows[at:end, :], rows[0:end, :], ROWS_BY_ROWS, preferred_element_type=F32
        ).astype(BF16)
        gram[at:end, 0:end] = term
        if at:
            gram[0:at, at:end] = term[:, :at].T


def gram_kernel(places, start, stop, *refs):
    count = len(places)
    groups = [refs[count * i : count * (i + 1)] for i in range(HALVES)]
    rows, gram, sems = refs[-3:]
    fetch(groups, places, rows, 0, sems)
    gram_strips(rows, gram, start, stop)


def add_gram(groups, places, start, stop, before):
    high, wide = groups[0][0].shape
    size = RING * high
    pieces = [group[place] for group in groups for place in places]
    return pl.pallas_call(
        functools.partial(gram_kernel, places, start, stop),
        out_shape=(
            jax.ShapeDtypeStruct((size, HALVES * wide), BF16),
            jax.ShapeDtypeStruct((size, size), BF16),
        ),
        in_specs=[ANYWHERE] * len(pieces) + [IN_VMEM] * len(before),
        out_specs=(IN_VMEM,) * 2,
        scratch_shapes=[pltpu.SemaphoreType.DMA((HALVES, PIECES))],
        input_output_aliases={len(pieces) + i: i for i in range(len(before))},
        compiler_params=pltpu.CompilerParams(vmem_limit_bytes=24 << 20),
        cost_estimate=cost(2 * (stop - start) * stop * wide * HALVES, 2 * len(pieces) * high * wide),
    )(*pieces, *before)


def finish_kernel(places, start, *refs):
    count = len(places)
    groups = [refs[count * i : count * (i + 1)] for i in range(HALVES)]
    refs = refs[count * HALVES :]
    moments, (_, _, out, rows, gram, sems) = refs[:HALVES], refs[HALVES:]
    fetch(groups, places, rows, 0, sems)
    size, cols = rows.shape
    own = out.shape[2]
    block = 0
    for moment in moments:
        for i in range(moment.shape[0]):
            out[block, 0] = moment[i]
            block += 1
    gram_strips(rows, gram, start, size)
    total = jnp.zeros((1, 1), F32)
    for at in range(0, size, LANE):
        term = gram[at : at + LANE, at : at + LANE].astype(F32)
        here = lax.broadcasted_iota(jnp.int32, term.shape, 0)
        there = lax.broadcasted_iota(jnp.int32, term.shape, 1)
        total = total + jnp.sum(jnp.where(here == there, term, 0.0), keepdims=True)
    inverse = 1.0 / (jnp.sqrt(total) + EPS_NORM)

    def times_gram(value):
        value = (value * inverse).astype(BF16)
        return jnp.dot(value, gram[...], preferred_element_type=F32) * inverse

    def poly(times, value):
        once = times(value)
        twice = times(once)
        return COEF_A * value + COEF_B * once + COEF_C * twice

    first = (lax.axis_index("fsdp") % 2) * own
    unit = (
        lax.broadcasted_iota(jnp.int32, (own, size), 0) + first
        == lax.broadcasted_iota(jnp.int32, (own, size), 1)
    ).astype(F32)
    value = poly(times_gram, unit)
    value = poly(lambda v: poly(times_gram, times_gram(poly(times_gram, v))), value)
    high = jnp.where(total < jnp.inf, value * inverse, 0.0).astype(BF16)
    for at in range(0, cols, 512):
        result = jnp.dot(high, rows[:, at : at + 512], preferred_element_type=F32).astype(BF16)
        for col in range(0, 512, LANE):
            out[(at + col) // LANE, 1] = result[:, col : col + LANE]


def finish(groups, places, start, moments, before):
    high, wide = groups[0][0].shape
    size = RING * high
    own = moments[0].shape[1]
    cols = HALVES * wide
    pieces = [group[place] for group in groups for place in places]
    inputs = len(pieces) + len(moments)
    return pl.pallas_call(
        functools.partial(finish_kernel, places, start),
        out_shape=(
            jax.ShapeDtypeStruct((cols // LANE, 2, own, LANE), BF16),
            jax.ShapeDtypeStruct((size, cols), BF16),
            jax.ShapeDtypeStruct((size, size), BF16),
        ),
        in_specs=[ANYWHERE] * len(pieces) + [IN_VMEM] * (len(moments) + 2),
        out_specs=(IN_VMEM,) * 3,
        scratch_shapes=[pltpu.SemaphoreType.DMA((HALVES, PIECES))],
        input_output_aliases={inputs: 1, inputs + 1: 2},
        compiler_params=pltpu.CompilerParams(vmem_limit_bytes=32 << 20),
        cost_estimate=cost(26 * own * size * size + size * size * cols, 2 * size * (size + cols)),
    )(*pieces, *moments, *before)[0]


def update_kernel(scale, returned, weights, moment_new, new_weights, update):
    moment_new[...] = returned[:, 0].astype(F32)
    direction = scale * returned[:, 1].astype(F32)
    update[...] = direction.astype(BF16)
    kept = weights[...].astype(F32) * (1.0 - LEARN_RATE * DECAY_RATE)
    new_weights[...] = (kept - LEARN_RATE * direction).astype(BF16)


def apply_update(returned, weights, scale):
    shape = weights.shape
    return pl.pallas_call(
        functools.partial(update_kernel, scale),
        out_shape=(
            jax.ShapeDtypeStruct(shape, F32),
            jax.ShapeDtypeStruct(shape, BF16),
            jax.ShapeDtypeStruct(shape, BF16),
        ),
        in_specs=[IN_VMEM] * 2,
        out_specs=(IN_VMEM,) * 3,
        compiler_params=pltpu.CompilerParams(vmem_limit_bytes=16 << 20),
    )(returned, weights)


def body(grads, momentum, weights):
    _, rows_dev, cols_dev = momentum.shape
    rows_total = rows_dev * lax.axis_size("fsdp")
    cols_total = cols_dev * lax.axis_size("dp")
    wide = cols_total // HALVES
    core = lax.axis_index("fsdp") % 2
    up1, down1 = pack(grads, momentum, wide, ((2, 0), (2, 1)), 59)
    up1, down1 = first_hop(up1, 1), first_hop(down1, -1)
    up2, down2 = pack(grads, momentum, wide, ((1, 1), (3, 0)), 59)
    up2, down2 = first_hop(up2, 1), first_hop(down2, -1)
    next_up, next_down, own0, own1 = pack(
        grads, momentum, wide, ((1, 0), (3, 1), (0, 0), (0, 1)), 48
    )
    up3, down3 = add_up(((next_up, up1), (next_down, down1)), False)
    up3, down3 = first_hop(up3, 1), first_hop(down3, -1)

    sums = add_up(((own0, down2, up3), (own1, up2, down3)), True)
    moments, groups = [], []
    for half in range(HALVES):
        parts = sums[SIDE * half : SIDE * (half + 1)]
        parts = [parts[0]] + [second_hop(parts[k], k) for k in (1, 2, 3)]
        moment, sent = combine(parts)
        moments.append(moment)
        groups.append(gather(sent, core))
    size = rows_total
    bounds = (size * 6 // 11, size * 9 // 11)
    before = add_gram(groups, range(0, 5), 0, bounds[0], ())
    before = add_gram(groups, range(5, 7), bounds[0], bounds[1], before)
    current = finish(groups, range(7, 9), bounds[1], moments, before)
    returned = lax.all_to_all(current, "dp", split_axis=0, concat_axis=0, tiled=True)
    return apply_update(returned, weights, 0.2 * math.sqrt(max(rows_total, cols_total)))


def solution(mesh):
    placed = (P("dp", None, "fsdp", None), P(None, "fsdp", "dp"), P(None, "fsdp", "dp"))
    return jax.shard_map(
        body,
        mesh=mesh,
        in_specs=placed,
        out_specs=(P(None, "fsdp", "dp"), P(None, "fsdp", "dp"), P(None, "fsdp", "dp")),
        check_vma=False,
    )
```

time: 448 us -> 130 us (0.29)
  the two profiles are of different devices: /device:TPU:64 before, /device:TPU:1 now
where the time goes in v1:
time: 130 us
  starting transfers between devices  58 us (45%)
  Pallas kernels  27.9 us (21%)
  waiting for transfers between devices  23.6 us (18%)
  blocking collectives  19.1 us (15%)
    ppermute x30, starting transfers between devices, move(): return lax.ppermute(value, ('dp', 'fsdp'), pairs)  58 us
    ppermute x30, waiting for transfers between devices, move(): return lax.ppermute(value, ('dp', 'fsdp'), pairs)  23.6 us
    all_to_all x1, blocking collectives, body(): lax.all_to_all(current, 'dp', split_axis=0, concat_axis=0, tiled=True)  19.1 us
    pallas_call x1, Pallas kernels, finish(): pl.pallas_call(functools.partial(finish_kernel, places, start), out_shape...  11.1 us
    pallas_call x3, Pallas kernels, pack(): pl.pallas_call(functools.partial(pack_kernel, wide, wanted), out_shape=(j...  8.06 us
    pallas_call x2, Pallas kernels, add_gram(): pl.pallas_call(functools.partial(gram_kernel, places, start, stop), out_s...  6.34 us
  transfers between devices with their start and end apart: 30, of which 12 were waited for; matrix products, arithmetic and copies ran while one was open for 0% of the time, Pallas kernels for 9%

profile of v1, /device:TPU:1, one launch (start us, length us, event | category | flops | bytes accessed | tf_op | source)
XLA Modules:
  0.0 129.6 jit_solution(6550313318942340804)
XLA Ops:
  0.6 0.0 copy-start
  0.6 2.9 %shard_map.60 = (bf16[4,88,1024]{2,1,0:T(8,128)(2,1)}, bf16[4,88,1024]{2,1,0:T(8,128)(2,1)}) custom-call(bf16[1,16,88,2048]{3,2,1,0:T(8,128)(2,1)} %grads.5, f32[16,88,128]{2,1,0:T(8,128)} %mom.5), custom_call_target="tpu_custom_call" | custom-call | bytes 2883584 | tf_op jit(solution)/shard_map/pallas_call | solution.py:99
  3.5 2.2 %collective-permute-start.1 = (bf16[4,88,1024]{2,1,0:T(8,128)(2,1)}, bf16[4,88,1024]{2,1,0:T(8,128)(2,1)S(1)}, u32[]{:S(2)}, u32[]{:S(2)}) collective-permute-start(bf16[4,88,1024]{2,1,0:T(8,128)(2,1)} %get-tuple-element.33), channel_id=1, source_target_pairs={{0,16},{1,65},{2,18},{3,67},{4,20},{5,69},{6,22},{7,71},{8,24},{9,... | collective-permute-start | bytes 2162696 | tf_op jit(solution)/shard_map/ppermute | solution.py:42
  5.8 1.5 %collective-permute-start.2 = (bf16[4,88,1024]{2,1,0:T(8,128)(2,1)}, bf16[4,88,1024]{2,1,0:T(8,128)(2,1)S(1)}, u32[]{:S(2)}, u32[]{:S(2)}) collective-permute-start(bf16[4,88,1024]{2,1,0:T(8,128)(2,1)} %get-tuple-element.35), channel_id=1, source_target_pairs={{0,48},{1,193},{2,50},{3,195},{4,52},{5,197},{6,54},{7,199},{8,56}... | collective-permute-start | bytes 2162696 | tf_op jit(solution)/shard_map/ppermute | solution.py:42
  7.3 2.8 %shard_map.59 = (bf16[4,88,1024]{2,1,0:T(8,128)(2,1)}, bf16[4,88,1024]{2,1,0:T(8,128)(2,1)}) custom-call(bf16[1,16,88,2048]{3,2,1,0:T(8,128)(2,1)} %grads.5, f32[16,88,128]{2,1,0:T(8,128)} %mom.5), custom_call_target="tpu_custom_call" | custom-call | bytes 2883584 | tf_op jit(solution)/shard_map/pallas_call | solution.py:99
  10.1 1.5 %collective-permute-start = (bf16[4,88,1024]{2,1,0:T(8,128)(2,1)}, bf16[4,88,1024]{2,1,0:T(8,128)(2,1)S(1)}, u32[]{:S(2)}, u32[]{:S(2)}) collective-permute-start(bf16[4,88,1024]{2,1,0:T(8,128)(2,1)} %get-tuple-element.31), channel_id=1, source_target_pairs={{0,48},{1,193},{2,50},{3,195},{4,52},{5,197},{6,54},{7,199},{8,56}... | collective-permute-start | bytes 2162696 | tf_op jit(solution)/shard_map/ppermute | solution.py:42
  11.6 0.1 collective-permute-start.4
  11.6 2.4 %shard_map.58 = (bf16[4,88,1024]{2,1,0:T(8,128)(2,1)S(1)}, bf16[4,88,1024]{2,1,0:T(8,128)(2,1)S(1)}, bf16[4,88,1024]{2,1,0:T(8,128)(2,1)S(1)}, bf16[4,88,1024]{2,1,0:T(8,128)(2,1)S(1)}) custom-call(bf16[1,16,88,2048]{3,2,1,0:T(8,128)(2,1)} %grads.5, f32[16,88,128]{2,1,0:T(8,128)S(1)} %copy-done), custom_call_target="tpu_custom_call" | custom-call | bytes 5767168 | tf_op jit(solution)/shard_map/pallas_call | solution.py:99
  14.0 2.4 %collective-permute-done.1.refs_1_ = bf16[4,88,1024]{2,1,0:T(8,128)(2,1)S(1)} collective-permute-done((bf16[4,88,1024]{2,1,0:T(8,128)(2,1)}, bf16[4,88,1024]{2,1,0:T(8,128)(2,1)S(1)}, u32[]{:S(2)}, u32[]{:S(2)}) %collective-permute-start.1) | collective-permute-done | bytes 720928 | tf_op jit(solution)/shard_map/ppermute | solution.py:42
  16.4 0.0 collective-permute-done.2.refs_3_
  16.4 0.3 shard_map.61
  16.7 1.4 %collective-permute-start.3 = (bf16[4,88,1024]{2,1,0:T(8,128)(2,1)S(1)}, bf16[4,88,1024]{2,1,0:T(8,128)(2,1)S(1)}, u32[]{:S(2)}, u32[]{:S(2)}) collective-permute-start(bf16[4,88,1024]{2,1,0:T(8,128)(2,1)S(1)} %get-tuple-element.36), channel_id=1, source_target_pairs={{0,16},{1,65},{2,18},{3,67},{4,20},{5,69},{6,22},{7,71},{8,24},{9,... | collective-permute-start | bytes 2162696 | tf_op jit(solution)/shard_map/ppermute | solution.py:42
  18.1 1.5 %collective-permute-start.5 = (bf16[4,88,1024]{2,1,0:T(8,128)(2,1)S(1)}, bf16[4,88,1024]{2,1,0:T(8,128)(2,1)S(1)}, u32[]{:S(2)}, u32[]{:S(2)}) collective-permute-start(bf16[4,88,1024]{2,1,0:T(8,128)(2,1)S(1)} %get-tuple-element.39), channel_id=1, source_target_pairs={{0,48},{1,193},{2,50},{3,195},{4,52},{5,197},{6,54},{7,199},{8,56}... | collective-permute-start | bytes 2162696 | tf_op jit(solution)/shard_map/ppermute | solution.py:42
  19.6 4.5 %collective-permute-done.refs_1_ = bf16[4,88,1024]{2,1,0:T(8,128)(2,1)S(1)} collective-permute-done((bf16[4,88,1024]{2,1,0:T(8,128)(2,1)}, bf16[4,88,1024]{2,1,0:T(8,128)(2,1)S(1)}, u32[]{:S(2)}, u32[]{:S(2)}) %collective-permute-start) | collective-permute-done | bytes 720928 | tf_op jit(solution)/shard_map/ppermute | solution.py:42
  24.1 0.0 collective-permute-done.4.refs_4_
  24.1 7.7 %collective-permute-done.3.refs_2_ = bf16[4,88,1024]{2,1,0:T(8,128)(2,1)S(1)} collective-permute-done((bf16[4,88,1024]{2,1,0:T(8,128)(2,1)S(1)}, bf16[4,88,1024]{2,1,0:T(8,128)(2,1)S(1)}, u32[]{:S(2)}, u32[]{:S(2)}) %collective-permute-start.3) | collective-permute-done | bytes 720928 | tf_op jit(solution)/shard_map/ppermute | solution.py:42
  31.8 0.0 collective-permute-done.5.refs_5_
  31.8 0.5 shard_map.62
  32.4 1.3 collective-permute-start.15
  33.7 2.5 %collective-permute-start.16 = (bf16[88,1024]{1,0:T(8,128)(2,1)S(1)}, bf16[88,1024]{1,0:T(8,128)(2,1)S(1)}, u32[]{:S(2)}, u32[]{:S(2)}) collective-permute-start(bf16[88,1024]{1,0:T(8,128)(2,1)S(1)} %get-tuple-element.47), channel_id=1, source_target_pairs={{0,128},{1,33},{2,130},{3,35},{4,132},{5,37},{6,134},{7,39},{8,136... | collective-permute-start | bytes 540680 | tf_op jit(solution)/shard_map/ppermute | solution.py:42
  36.1 1.2 collective-permute-start.17
  37.3 0.3 collective-permute-start.6
  37.6 0.9 collective-permute-start.7
  38.4 0.0 collective-permute-done.15.part1
  38.5 1.5 %collective-permute-start.8 = (bf16[88,1024]{1,0:T(8,128)(2,1)S(1)}, bf16[88,1024]{1,0:T(8,128)(2,1)S(1)}, u32[]{:S(2)}, u32[]{:S(2)}) collective-permute-start(bf16[88,1024]{1,0:T(8,128)(2,1)S(1)} %get-tuple-element.43), channel_id=1, source_target_pairs={{0,192},{1,49},{2,194},{3,51},{4,196},{5,53},{6,198},{7,55},{8,200... | collective-permute-start | bytes 540680 | tf_op jit(solution)/shard_map/ppermute | solution.py:42
  40.0 0.9 collective-permute-done.16.part2
  40.9 0.1 shard_map.64
  41.1 4.3 %collective-permute-start.18 = (bf16[88,1024]{1,0:T(8,128)(2,1)S(1)}, bf16[88,1024]{1,0:T(8,128)(2,1)S(1)}, u32[]{:S(2)}, u32[]{:S(2)}) collective-permute-start(bf16[88,1024]{1,0:T(8,128)(2,1)S(1)} %get-tuple-element.49), channel_id=1, source_target_pairs={{0,1},{1,0},{2,3},{3,2},{4,5},{5,4},{6,7},{7,6},{8,9},{9,8},{10,11... | collective-permute-start | bytes 540680 | tf_op jit(solution)/shard_map/ppermute | solution.py:42
  45.3 0.0 collective-permute-done.7.part2
  45.3 0.3 collective-permute-done.8.part3
  45.7 0.1 shard_map.63
  45.8 0.0 copy-start.2
  45.8 4.2 %collective-permute-start.9 = (bf16[88,1024]{1,0:T(8,128)(2,1)S(1)}, bf16[88,1024]{1,0:T(8,128)(2,1)S(1)}, u32[]{:S(2)}, u32[]{:S(2)}) collective-permute-start(bf16[88,1024]{1,0:T(8,128)(2,1)S(1)} %get-tuple-element.44), channel_id=1, source_target_pairs={{0,1},{1,0},{2,3},{3,2},{4,5},{5,4},{6,7},{7,6},{8,9},{9,8},{10,11... | collective-permute-start | bytes 540680 | tf_op jit(solution)/shard_map/ppermute | solution.py:42
  50.1 5.6 %collective-permute-start.19 = (bf16[176,1024]{1,0:T(8,128)(2,1)S(1)}, bf16[176,1024]{1,0:T(8,128)(2,1)S(1)}, u32[]{:S(2)}, u32[]{:S(2)}) collective-permute-start(bf16[176,1024]{1,0:T(8,128)(2,1)S(1)} %pad_maximum_fusion.1.refs_5_), channel_id=1, source_target_pairs={{0,2},{1,15},{2,4},{3,1},{4,6},{5,3},{6,8},{7,5},{8,10},{9,7},{10,... | collective-permute-start | bytes 1081352 | tf_op jit(solution)/shard_map/ppermute | solution.py:42
  55.7 0.8 collective-permute-start.10
  56.6 3.5 %collective-permute-done.19.refs_6_ = bf16[176,1024]{1,0:T(8,128)(2,1)S(1)} collective-permute-done((bf16[176,1024]{1,0:T(8,128)(2,1)S(1)}, bf16[176,1024]{1,0:T(8,128)(2,1)S(1)}, u32[]{:S(2)}, u32[]{:S(2)}) %collective-permute-start.19) | collective-permute-done | bytes 360480 | tf_op jit(solution)/shard_map/ppermute | solution.py:42
  60.0 3.1 %collective-permute-start.20 = (bf16[176,1024]{1,0:T(8,128)(2,1)S(1)}, bf16[176,1024]{1,0:T(8,128)(2,1)S(1)}, u32[]{:S(2)}, u32[]{:S(2)}) collective-permute-start(bf16[176,1024]{1,0:T(8,128)(2,1)S(1)} %collective-permute-done.19.refs_6_), channel_id=1, source_target_pairs={{0,2},{1,15},{2,4},{3,1},{4,6},{5,3},{6,8},{7,5},{8,10},{9,7},{10,... | collective-permute-start | bytes 1081352 | tf_op jit(solution)/shard_map/ppermute | solution.py:42
  63.2 0.7 collective-permute-done.10.refs_1_
  63.9 3.1 %collective-permute-start.11 = (bf16[176,1024]{1,0:T(8,128)(2,1)S(1)}, bf16[176,1024]{1,0:T(8,128)(2,1)S(1)}, u32[]{:S(2)}, u32[]{:S(2)}) collective-permute-start(bf16[176,1024]{1,0:T(8,128)(2,1)S(1)} %collective-permute-done.10.refs_1_), channel_id=1, source_target_pairs={{0,2},{1,15},{2,4},{3,1},{4,6},{5,3},{6,8},{7,5},{8,10},{9,7},{10,... | collective-permute-start | bytes 1081352 | tf_op jit(solution)/shard_map/ppermute | solution.py:42
  67.0 0.7 collective-permute-done.20.refs_8_
  67.8 3.1 %collective-permute-start.21 = (bf16[176,1024]{1,0:T(8,128)(2,1)S(1)}, bf16[176,1024]{1,0:T(8,128)(2,1)S(1)}, u32[]{:S(2)}, u32[]{:S(2)}) collective-permute-start(bf16[176,1024]{1,0:T(8,128)(2,1)S(1)} %collective-permute-done.20.refs_8_), channel_id=1, source_target_pairs={{0,2},{1,15},{2,4},{3,1},{4,6},{5,3},{6,8},{7,5},{8,10},{9,7},{10,... | collective-permute-start | bytes 1081352 | tf_op jit(solution)/shard_map/ppermute | solution.py:42
  70.9 0.7 collective-permute-done.11.refs_3_
  71.6 3.1 %collective-permute-start.12 = (bf16[176,1024]{1,0:T(8,128)(2,1)S(1)}, bf16[176,1024]{1,0:T(8,128)(2,1)S(1)}, u32[]{:S(2)}, u32[]{:S(2)}) collective-permute-start(bf16[176,1024]{1,0:T(8,128)(2,1)S(1)} %collective-permute-done.11.refs_3_), channel_id=1, source_target_pairs={{0,2},{1,15},{2,4},{3,1},{4,6},{5,3},{6,8},{7,5},{8,10},{9,7},{10,... | collective-permute-start | bytes 1081352 | tf_op jit(solution)/shard_map/ppermute | solution.py:42
  74.7 0.0 collective-permute-start.28
  74.8 0.5 collective-permute-start.26
  75.3 0.2 collective-permute-done.21.refs_2_
  75.5 3.7 %collective-permute-start.27 = (bf16[176,1024]{1,0:T(8,128)(2,1)S(1)}, bf16[176,1024]{1,0:T(8,128)(2,1)S(1)}, u32[]{:S(2)}, u32[]{:S(2)}) collective-permute-start(bf16[176,1024]{1,0:T(8,128)(2,1)S(1)} %collective-permute-done.11.refs_3_), channel_id=1, source_target_pairs={{0,1},{1,0},{2,3},{3,2},{4,5},{5,4},{6,7},{7,6},{8,9},{9,8},{10,11... | collective-permute-start | bytes 1081352 | tf_op jit(solution)/shard_map/ppermute | solution.py:42
  79.2 0.2 collective-permute-done.12.refs_0_
  79.4 3.1 %collective-permute-start.22 = (bf16[176,512]{1,0:T(8,128)(2,1)S(1)}, bf16[176,512]{1,0:T(8,128)(2,1)S(1)}, u32[]{:S(2)}, u32[]{:S(2)}) collective-permute-start(bf16[176,512]{1,0:T(8,128)(2,1)S(1)} %constant_dynamic-slice_fusion), channel_id=1, source_target_pairs={{0,2},{1,15},{2,4},{3,1},{4,6},{5,3},{6,8},{7,5},{8,10},{9,7},{10,... | collective-permute-start | bytes 540680 | tf_op jit(solution)/shard_map/ppermute | solution.py:42
  82.5 0.0 collective-permute-done.28.refs_7_
  82.5 0.1 collective-permute-start.13
  82.6 0.0 collective-permute-done.26.refs_2_
  82.6 0.6 collective-permute-start.25
  83.2 0.1 collective-permute-start.24
  83.4 1.6 %collective-permute-done.22.refs_2_ = bf16[176,512]{1,0:T(8,128)(2,1)S(1)} collective-permute-done((bf16[176,512]{1,0:T(8,128)(2,1)S(1)}, bf16[176,512]{1,0:T(8,128)(2,1)S(1)}, u32[]{:S(2)}, u32[]{:S(2)}) %collective-permute-start.22) | collective-permute-done | bytes 180256 | tf_op jit(solution)/shard_map/ppermute | solution.py:42
  84.9 4.8 %collective-permute-start.23 = (bf16[176,512]{1,0:T(8,128)(2,1)S(1)}, bf16[176,512]{1,0:T(8,128)(2,1)S(1)}, u32[]{:S(2)}, u32[]{:S(2)}) collective-permute-start(bf16[176,512]{1,0:T(8,128)(2,1)S(1)} %collective-permute-done.22.refs_2_), channel_id=1, source_target_pairs={{0,1},{1,0},{2,3},{3,2},{4,5},{5,4},{6,7},{7,6},{8,9},{9,8},{10,11... | collective-permute-start | bytes 540680 | tf_op jit(solution)/shard_map/ppermute | solution.py:42
  89.7 1.9 %collective-permute-start.14 = (bf16[176,512]{1,0:T(8,128)(2,1)S(1)}, bf16[176,512]{1,0:T(8,128)(2,1)S(1)}, u32[]{:S(2)}, u32[]{:S(2)}) collective-permute-start(bf16[176,512]{1,0:T(8,128)(2,1)S(1)} %collective-permute-done.13.refs_0_), channel_id=1, source_target_pairs={{0,1},{1,0},{2,3},{3,2},{4,5},{5,4},{6,7},{7,6},{8,9},{9,8},{10,11... | collective-permute-start | bytes 540680 | tf_op jit(solution)/shard_map/ppermute | solution.py:42
  91.7 3.3 %shard_map.65 = (bf16[1408,2048]{1,0:T(8,128)(2,1)S(1)}, bf16[1408,1408]{1,0:T(8,128)(2,1)S(1)}) custom-call(bf16[176,1024]{1,0:T(8,128)(2,1)S(1)} %pad_maximum_fusion.refs_0_, bf16[176,1024]{1,0:T(8,128)(2,1)S(1)} %collective-permute-done.10.refs_1_, bf16[176,1024]{1,0:T(8,128)(2,1)} %collective-permute-done.26.refs_2_, ...), custom_call_target="tpu_custom_call" | custom-call | flops 2415919104 | bytes 3604480 | tf_op jit(solution)/shard_map/pallas_call | solution.py:223
  95.0 0.0 copy-start.3
  95.0 3.0 %shard_map.66 = (bf16[1408,2048]{1,0:T(8,128)(2,1)S(1)}, bf16[1408,1408]{1,0:T(8,128)(2,1)S(1)}) custom-call(bf16[176,1024]{1,0:T(8,128)(2,1)S(1)} %collective-permute-done.12.refs_0_, bf16[176,1024]{1,0:T(8,128)(2,1)S(1)} %collective-permute-done.24.refs_1_, ...), custom_call_target="tpu_custom_call", output_to_operand_aliasing={{0}: (4, {}), {1}: (5, {})} | custom-call | flops 1811939328 | bytes 1441792 | tf_op jit(solution)/shard_map/pallas_call | solution.py:223
  98.1 0.0 copy-start.1
  98.1 11.1 %shard_map.67 = (bf16[16,2,88,128]{3,2,1,0:T(8,128)(2,1)S(1)}, bf16[1408,2048]{1,0:T(8,128)(2,1)S(1)}, bf16[1408,1408]{1,0:T(8,128)(2,1)S(1)}) custom-call(bf16[176,512]{1,0:T(8,128)(2,1)S(1)} %collective-permute-done.13.refs_0_, bf16[176,512]{1,0:T(8,128)(2,1)S(1)} %collective-permute-done.14.refs_1_, ...), custom_call_target="tpu_custom_call", output_to_operand_aliasing={{1}: (6, {}), {2}: (7, {})} | custom-call | flops 8595963904 | bytes 9732096 | tf_op jit(solution)/shard_map/pallas_call | solution.py:290
  109.2 19.1 %all_to_all.5.returned = bf16[16,2,88,128]{3,2,1,0:T(8,128)(2,1)S(1)} all-to-all(bf16[16,2,88,128]{3,2,1,0:T(8,128)(2,1)S(1)} %get-tuple-element.56), channel_id=1, replica_groups=mesh['dp'=16,'fsdp'=16] {'dp'}, dimensions={0} | all-to-all | bytes 1441792 | tf_op jit(solution)/shard_map/all_to_all | solution.py:358
  128.4 1.2 shard_map.68
  (22 shorter events, 0.2 us)
Async XLA Ops:
  0.6 11.0 %copy-start = (f32[16,88,128]{2,1,0:T(8,128)S(1)}, f32[16,88,128]{2,1,0:T(8,128)}, u32[]{:S(2)}) copy-start(f32[16,88,128]{2,1,0:T(8,128)} %mom.5) | copy-start | bytes 2162692
  3.5 12.8 %collective-permute-start.1 = (bf16[4,88,1024]{2,1,0:T(8,128)(2,1)}, bf16[4,88,1024]{2,1,0:T(8,128)(2,1)S(1)}, u32[]{:S(2)}, u32[]{:S(2)}) collective-permute-start(bf16[4,88,1024]{2,1,0:T(8,128)(2,1)} %get-tuple-element.33), channel_id=1, source_target_pairs={{0,16},{1,65},{2,18},{3,67},{4,20},{5,69},{6,22},{7,71},{8,24},{9,... | collective-permute-start | bytes 2162696 | tf_op jit(solution)/shard_map/ppermute | solution.py:42
  5.8 10.6 %collective-permute-start.2 = (bf16[4,88,1024]{2,1,0:T(8,128)(2,1)}, bf16[4,88,1024]{2,1,0:T(8,128)(2,1)S(1)}, u32[]{:S(2)}, u32[]{:S(2)}) collective-permute-start(bf16[4,88,1024]{2,1,0:T(8,128)(2,1)} %get-tuple-element.35), channel_id=1, source_target_pairs={{0,48},{1,193},{2,50},{3,195},{4,52},{5,197},{6,54},{7,199},{8,56}... | collective-permute-start | bytes 2162696 | tf_op jit(solution)/shard_map/ppermute | solution.py:42
  10.1 14.0 %collective-permute-start = (bf16[4,88,1024]{2,1,0:T(8,128)(2,1)}, bf16[4,88,1024]{2,1,0:T(8,128)(2,1)S(1)}, u32[]{:S(2)}, u32[]{:S(2)}) collective-permute-start(bf16[4,88,1024]{2,1,0:T(8,128)(2,1)} %get-tuple-element.31), channel_id=1, source_target_pairs={{0,48},{1,193},{2,50},{3,195},{4,52},{5,197},{6,54},{7,199},{8,56}... | collective-permute-start | bytes 2162696 | tf_op jit(solution)/shard_map/ppermute | solution.py:42
  11.6 12.6 %collective-permute-start.4 = (bf16[4,88,1024]{2,1,0:T(8,128)(2,1)}, bf16[4,88,1024]{2,1,0:T(8,128)(2,1)S(1)}, u32[]{:S(2)}, u32[]{:S(2)}) collective-permute-start(bf16[4,88,1024]{2,1,0:T(8,128)(2,1)} %get-tuple-element.38), channel_id=1, source_target_pairs={{0,16},{1,65},{2,18},{3,67},{4,20},{5,69},{6,22},{7,71},{8,24},{9,... | collective-permute-start | bytes 2162696 | tf_op jit(solution)/shard_map/ppermute | solution.py:42
  16.7 15.1 %collective-permute-start.3 = (bf16[4,88,1024]{2,1,0:T(8,128)(2,1)S(1)}, bf16[4,88,1024]{2,1,0:T(8,128)(2,1)S(1)}, u32[]{:S(2)}, u32[]{:S(2)}) collective-permute-start(bf16[4,88,1024]{2,1,0:T(8,128)(2,1)S(1)} %get-tuple-element.36), channel_id=1, source_target_pairs={{0,16},{1,65},{2,18},{3,67},{4,20},{5,69},{6,22},{7,71},{8,24},{9,... | collective-permute-start | bytes 2162696 | tf_op jit(solution)/shard_map/ppermute | solution.py:42
  18.1 13.8 %collective-permute-start.5 = (bf16[4,88,1024]{2,1,0:T(8,128)(2,1)S(1)}, bf16[4,88,1024]{2,1,0:T(8,128)(2,1)S(1)}, u32[]{:S(2)}, u32[]{:S(2)}) collective-permute-start(bf16[4,88,1024]{2,1,0:T(8,128)(2,1)S(1)} %get-tuple-element.39), channel_id=1, source_target_pairs={{0,48},{1,193},{2,50},{3,195},{4,52},{5,197},{6,54},{7,199},{8,56}... | collective-permute-start | bytes 2162696 | tf_op jit(solution)/shard_map/ppermute | solution.py:42
  32.4 6.1 %collective-permute-start.15 = (bf16[88,1024]{1,0:T(8,128)(2,1)S(1)}, bf16[88,1024]{1,0:T(8,128)(2,1)S(1)}, u32[]{:S(2)}, u32[]{:S(2)}) collective-permute-start(bf16[88,1024]{1,0:T(8,128)(2,1)S(1)} %get-tuple-element.46), channel_id=1, source_target_pairs={{0,64},{1,17},{2,66},{3,19},{4,68},{5,21},{6,70},{7,23},{8,72},{9,... | collective-permute-start | bytes 540680 | tf_op jit(solution)/shard_map/ppermute | solution.py:42
  33.7 7.3 %collective-permute-start.16 = (bf16[88,1024]{1,0:T(8,128)(2,1)S(1)}, bf16[88,1024]{1,0:T(8,128)(2,1)S(1)}, u32[]{:S(2)}, u32[]{:S(2)}) collective-permute-start(bf16[88,1024]{1,0:T(8,128)(2,1)S(1)} %get-tuple-element.47), channel_id=1, source_target_pairs={{0,128},{1,33},{2,130},{3,35},{4,132},{5,37},{6,134},{7,39},{8,136... | collective-permute-start | bytes 540680 | tf_op jit(solution)/shard_map/ppermute | solution.py:42
  36.1 4.8 %collective-permute-start.17 = (bf16[88,1024]{1,0:T(8,128)(2,1)S(1)}, bf16[88,1024]{1,0:T(8,128)(2,1)S(1)}, u32[]{:S(2)}, u32[]{:S(2)}) collective-permute-start(bf16[88,1024]{1,0:T(8,128)(2,1)S(1)} %get-tuple-element.48), channel_id=1, source_target_pairs={{0,192},{1,49},{2,194},{3,51},{4,196},{5,53},{6,198},{7,55},{8,200... | collective-permute-start | bytes 540680 | tf_op jit(solution)/shard_map/ppermute | solution.py:42
  37.3 8.1 %collective-permute-start.6 = (bf16[88,1024]{1,0:T(8,128)(2,1)S(1)}, bf16[88,1024]{1,0:T(8,128)(2,1)S(1)}, u32[]{:S(2)}, u32[]{:S(2)}) collective-permute-start(bf16[88,1024]{1,0:T(8,128)(2,1)S(1)} %get-tuple-element.41), channel_id=1, source_target_pairs={{0,64},{1,17},{2,66},{3,19},{4,68},{5,21},{6,70},{7,23},{8,72},{9,... | collective-permute-start | bytes 540680 | tf_op jit(solution)/shard_map/ppermute | solution.py:42
  37.6 7.8 %collective-permute-start.7 = (bf16[88,1024]{1,0:T(8,128)(2,1)S(1)}, bf16[88,1024]{1,0:T(8,128)(2,1)S(1)}, u32[]{:S(2)}, u32[]{:S(2)}) collective-permute-start(bf16[88,1024]{1,0:T(8,128)(2,1)S(1)} %get-tuple-element.42), channel_id=1, source_target_pairs={{0,128},{1,33},{2,130},{3,35},{4,132},{5,37},{6,134},{7,39},{8,136... | collective-permute-start | bytes 540680 | tf_op jit(solution)/shard_map/ppermute | solution.py:42
  38.5 7.2 %collective-permute-start.8 = (bf16[88,1024]{1,0:T(8,128)(2,1)S(1)}, bf16[88,1024]{1,0:T(8,128)(2,1)S(1)}, u32[]{:S(2)}, u32[]{:S(2)}) collective-permute-start(bf16[88,1024]{1,0:T(8,128)(2,1)S(1)} %get-tuple-element.43), channel_id=1, source_target_pairs={{0,192},{1,49},{2,194},{3,51},{4,196},{5,53},{6,198},{7,55},{8,200... | collective-permute-start | bytes 540680 | tf_op jit(solution)/shard_map/ppermute | solution.py:42
  41.1 8.9 %collective-permute-start.18 = (bf16[88,1024]{1,0:T(8,128)(2,1)S(1)}, bf16[88,1024]{1,0:T(8,128)(2,1)S(1)}, u32[]{:S(2)}, u32[]{:S(2)}) collective-permute-start(bf16[88,1024]{1,0:T(8,128)(2,1)S(1)} %get-tuple-element.49), channel_id=1, source_target_pairs={{0,1},{1,0},{2,3},{3,2},{4,5},{5,4},{6,7},{7,6},{8,9},{9,8},{10,11... | collective-permute-start | bytes 540680 | tf_op jit(solution)/shard_map/ppermute | solution.py:42
  45.8 4.2 %copy-start.2 = (bf16[8,88,128]{2,1,0:T(8,128)(2,1)}, bf16[8,88,128]{2,1,0:T(8,128)(2,1)S(1)}, u32[]{:S(2)}) copy-start(bf16[8,88,128]{2,1,0:T(8,128)(2,1)S(1)} %get-tuple-element.50.refs_4_) | copy-start | bytes 540676
  45.8 9.9 %collective-permute-start.9 = (bf16[88,1024]{1,0:T(8,128)(2,1)S(1)}, bf16[88,1024]{1,0:T(8,128)(2,1)S(1)}, u32[]{:S(2)}, u32[]{:S(2)}) collective-permute-start(bf16[88,1024]{1,0:T(8,128)(2,1)S(1)} %get-tuple-element.44), channel_id=1, source_target_pairs={{0,1},{1,0},{2,3},{3,2},{4,5},{5,4},{6,7},{7,6},{8,9},{9,8},{10,11... | collective-permute-start | bytes 540680 | tf_op jit(solution)/shard_map/ppermute | solution.py:42
  50.1 10.0 %collective-permute-start.19 = (bf16[176,1024]{1,0:T(8,128)(2,1)S(1)}, bf16[176,1024]{1,0:T(8,128)(2,1)S(1)}, u32[]{:S(2)}, u32[]{:S(2)}) collective-permute-start(bf16[176,1024]{1,0:T(8,128)(2,1)S(1)} %pad_maximum_fusion.1.refs_5_), channel_id=1, source_target_pairs={{0,2},{1,15},{2,4},{3,1},{4,6},{5,3},{6,8},{7,5},{8,10},{9,7},{10,... | collective-permute-start | bytes 1081352 | tf_op jit(solution)/shard_map/ppermute | solution.py:42
  55.7 8.2 %collective-permute-start.10 = (bf16[176,1024]{1,0:T(8,128)(2,1)S(1)}, bf16[176,1024]{1,0:T(8,128)(2,1)S(1)}, u32[]{:S(2)}, u32[]{:S(2)}) collective-permute-start(bf16[176,1024]{1,0:T(8,128)(2,1)S(1)} %pad_maximum_fusion.refs_0_), channel_id=1, source_target_pairs={{0,2},{1,15},{2,4},{3,1},{4,6},{5,3},{6,8},{7,5},{8,10},{9,7},{10,... | collective-permute-start | bytes 1081352 | tf_op jit(solution)/shard_map/ppermute | solution.py:42
  60.0 7.7 %collective-permute-start.20 = (bf16[176,1024]{1,0:T(8,128)(2,1)S(1)}, bf16[176,1024]{1,0:T(8,128)(2,1)S(1)}, u32[]{:S(2)}, u32[]{:S(2)}) collective-permute-start(bf16[176,1024]{1,0:T(8,128)(2,1)S(1)} %collective-permute-done.19.refs_6_), channel_id=1, source_target_pairs={{0,2},{1,15},{2,4},{3,1},{4,6},{5,3},{6,8},{7,5},{8,10},{9,7},{10,... | collective-permute-start | bytes 1081352 | tf_op jit(solution)/shard_map/ppermute | solution.py:42
  63.9 7.7 %collective-permute-start.11 = (bf16[176,1024]{1,0:T(8,128)(2,1)S(1)}, bf16[176,1024]{1,0:T(8,128)(2,1)S(1)}, u32[]{:S(2)}, u32[]{:S(2)}) collective-permute-start(bf16[176,1024]{1,0:T(8,128)(2,1)S(1)} %collective-permute-done.10.refs_1_), channel_id=1, source_target_pairs={{0,2},{1,15},{2,4},{3,1},{4,6},{5,3},{6,8},{7,5},{8,10},{9,7},{10,... | collective-permute-start | bytes 1081352 | tf_op jit(solution)/shard_map/ppermute | solution.py:42
  67.8 7.7 %collective-permute-start.21 = (bf16[176,1024]{1,0:T(8,128)(2,1)S(1)}, bf16[176,1024]{1,0:T(8,128)(2,1)S(1)}, u32[]{:S(2)}, u32[]{:S(2)}) collective-permute-start(bf16[176,1024]{1,0:T(8,128)(2,1)S(1)} %collective-permute-done.20.refs_8_), channel_id=1, source_target_pairs={{0,2},{1,15},{2,4},{3,1},{4,6},{5,3},{6,8},{7,5},{8,10},{9,7},{10,... | collective-permute-start | bytes 1081352 | tf_op jit(solution)/shard_map/ppermute | solution.py:42
  71.6 7.7 %collective-permute-start.12 = (bf16[176,1024]{1,0:T(8,128)(2,1)S(1)}, bf16[176,1024]{1,0:T(8,128)(2,1)S(1)}, u32[]{:S(2)}, u32[]{:S(2)}) collective-permute-start(bf16[176,1024]{1,0:T(8,128)(2,1)S(1)} %collective-permute-done.11.refs_3_), channel_id=1, source_target_pairs={{0,2},{1,15},{2,4},{3,1},{4,6},{5,3},{6,8},{7,5},{8,10},{9,7},{10,... | collective-permute-start | bytes 1081352 | tf_op jit(solution)/shard_map/ppermute | solution.py:42
  74.7 7.7 %collective-permute-start.28 = (bf16[176,1024]{1,0:T(8,128)(2,1)S(1)}, bf16[176,1024]{1,0:T(8,128)(2,1)S(1)}, u32[]{:S(2)}, u32[]{:S(2)}) collective-permute-start(bf16[176,1024]{1,0:T(8,128)(2,1)S(1)} %collective-permute-done.19.refs_6_), channel_id=1, source_target_pairs={{0,1},{1,0},{2,3},{3,2},{4,5},{5,4},{6,7},{7,6},{8,9},{9,8},{10,11... | collective-permute-start | bytes 1081352 | tf_op jit(solution)/shard_map/ppermute | solution.py:42
  74.8 7.8 %collective-permute-start.26 = (bf16[176,1024]{1,0:T(8,128)(2,1)S(1)}, bf16[176,1024]{1,0:T(8,128)(2,1)}, u32[]{:S(2)}, u32[]{:S(2)}) collective-permute-start(bf16[176,1024]{1,0:T(8,128)(2,1)S(1)} %collective-permute-done.10.refs_1_), channel_id=1, source_target_pairs={{0,1},{1,0},{2,3},{3,2},{4,5},{5,4},{6,7},{7,6},{8,9},{9,8},{10,11... | collective-permute-start | bytes 1081352 | tf_op jit(solution)/shard_map/ppermute | solution.py:42
  75.3 8.0 %collective-permute-start.29 = (bf16[176,1024]{1,0:T(8,128)(2,1)S(1)}, bf16[176,1024]{1,0:T(8,128)(2,1)}, u32[]{:S(2)}, u32[]{:S(2)}) collective-permute-start(bf16[176,1024]{1,0:T(8,128)(2,1)S(1)} %collective-permute-done.20.refs_8_), channel_id=1, source_target_pairs={{0,1},{1,0},{2,3},{3,2},{4,5},{5,4},{6,7},{7,6},{8,9},{9,8},{10,11... | collective-permute-start | bytes 1081352 | tf_op jit(solution)/shard_map/ppermute | solution.py:42
  75.5 16.2 %collective-permute-start.27 = (bf16[176,1024]{1,0:T(8,128)(2,1)S(1)}, bf16[176,1024]{1,0:T(8,128)(2,1)S(1)}, u32[]{:S(2)}, u32[]{:S(2)}) collective-permute-start(bf16[176,1024]{1,0:T(8,128)(2,1)S(1)} %collective-permute-done.11.refs_3_), channel_id=1, source_target_pairs={{0,1},{1,0},{2,3},{3,2},{4,5},{5,4},{6,7},{7,6},{8,9},{9,8},{10,11... | collective-permute-start | bytes 1081352 | tf_op jit(solution)/shard_map/ppermute | solution.py:42
  79.4 5.6 %collective-permute-start.22 = (bf16[176,512]{1,0:T(8,128)(2,1)S(1)}, bf16[176,512]{1,0:T(8,128)(2,1)S(1)}, u32[]{:S(2)}, u32[]{:S(2)}) collective-permute-start(bf16[176,512]{1,0:T(8,128)(2,1)S(1)} %constant_dynamic-slice_fusion), channel_id=1, source_target_pairs={{0,2},{1,15},{2,4},{3,1},{4,6},{5,3},{6,8},{7,5},{8,10},{9,7},{10,... | collective-permute-start | bytes 540680 | tf_op jit(solution)/shard_map/ppermute | solution.py:42
  82.5 7.2 %collective-permute-start.13 = (bf16[176,512]{1,0:T(8,128)(2,1)S(1)}, bf16[176,512]{1,0:T(8,128)(2,1)S(1)}, u32[]{:S(2)}, u32[]{:S(2)}) collective-permute-start(bf16[176,512]{1,0:T(8,128)(2,1)S(1)} %constant_dynamic-slice_fusion.1), channel_id=1, source_target_pairs={{0,2},{1,15},{2,4},{3,1},{4,6},{5,3},{6,8},{7,5},{8,10},{9,7},{10,... | collective-permute-start | bytes 540680 | tf_op jit(solution)/shard_map/ppermute | solution.py:42
  82.6 12.4 %collective-permute-start.25 = (bf16[176,1024]{1,0:T(8,128)(2,1)S(1)}, bf16[176,1024]{1,0:T(8,128)(2,1)S(1)}, u32[]{:S(2)}, u32[]{:S(2)}) collective-permute-start(bf16[176,1024]{1,0:T(8,128)(2,1)S(1)} %collective-permute-done.21.refs_2_), channel_id=1, source_target_pairs={{0,1},{1,0},{2,3},{3,2},{4,5},{5,4},{6,7},{7,6},{8,9},{9,8},{10,11... | collective-permute-start | bytes 1081352 | tf_op jit(solution)/shard_map/ppermute | solution.py:42
  83.2 11.8 %collective-permute-start.24 = (bf16[176,1024]{1,0:T(8,128)(2,1)S(1)}, bf16[176,1024]{1,0:T(8,128)(2,1)S(1)}, u32[]{:S(2)}, u32[]{:S(2)}) collective-permute-start(bf16[176,1024]{1,0:T(8,128)(2,1)S(1)} %collective-permute-done.12.refs_0_), channel_id=1, source_target_pairs={{0,1},{1,0},{2,3},{3,2},{4,5},{5,4},{6,7},{7,6},{8,9},{9,8},{10,11... | collective-permute-start | bytes 1081352 | tf_op jit(solution)/shard_map/ppermute | solution.py:42
  84.9 13.1 %collective-permute-start.23 = (bf16[176,512]{1,0:T(8,128)(2,1)S(1)}, bf16[176,512]{1,0:T(8,128)(2,1)S(1)}, u32[]{:S(2)}, u32[]{:S(2)}) collective-permute-start(bf16[176,512]{1,0:T(8,128)(2,1)S(1)} %collective-permute-done.22.refs_2_), channel_id=1, source_target_pairs={{0,1},{1,0},{2,3},{3,2},{4,5},{5,4},{6,7},{7,6},{8,9},{9,8},{10,11... | collective-permute-start | bytes 540680 | tf_op jit(solution)/shard_map/ppermute | solution.py:42
  89.7 8.3 %collective-permute-start.14 = (bf16[176,512]{1,0:T(8,128)(2,1)S(1)}, bf16[176,512]{1,0:T(8,128)(2,1)S(1)}, u32[]{:S(2)}, u32[]{:S(2)}) collective-permute-start(bf16[176,512]{1,0:T(8,128)(2,1)S(1)} %collective-permute-done.13.refs_0_), channel_id=1, source_target_pairs={{0,1},{1,0},{2,3},{3,2},{4,5},{5,4},{6,7},{7,6},{8,9},{9,8},{10,11... | collective-permute-start | bytes 540680 | tf_op jit(solution)/shard_map/ppermute | solution.py:42
  95.0 3.1 %copy-start.3 = (bf16[8,88,128]{2,1,0:T(8,128)(2,1)S(1)}, bf16[8,88,128]{2,1,0:T(8,128)(2,1)}, u32[]{:S(2)}) copy-start(bf16[8,88,128]{2,1,0:T(8,128)(2,1)} %copy-done.2) | copy-start | bytes 540676
  98.1 30.3 %copy-start.1 = (bf16[16,88,128]{2,1,0:T(8,128)(2,1)S(1)}, bf16[16,88,128]{2,1,0:T(8,128)(2,1)}, u32[]{:S(2)}) copy-start(bf16[16,88,128]{2,1,0:T(8,128)(2,1)} %weights.1) | copy-start | bytes 1081348
